TPU v7x, 32 devices: a whole 2x2x4 slice. The times are simulated.
32 devices in a mesh: dp: 16 (over z, y, x), query: 2 (over core).
Axes of the slice: x: 2, y: 2, z: 4, core: 2. Of those that a mesh axis runs over, the one named last changes fastest.
Arguments:
- hidden_acts: bfloat16 [2048, 4, 14336], P(('dp', 'query')), may hold values from -5 to 5
- out_grads: bfloat16 [2048, 4, 4096], P(('dp', 'query')), may hold values from -5 to 5
- loss_mask: int32 [2048, 4], P(('dp', 'query')), may hold values from 0 to 1, as said below
- proj_in: bfloat16 [32, 14336], replicated, may hold values from -0.046875 to 0.046875
- proj_out: bfloat16 [32, 4096], replicated, may hold values from -0.09375 to 0.09375
- queries: float32 [256, 1024], P('query'), may hold values from -0.3125 to 0.3125
Outputs:
- scores: float32 [2048, 256], P(('dp', 'query'))
Inputs may be any that keep to these rules, and one draw needn't show every extreme that they name: `loss_mask`: the first token of every sequence counts.
All inputs are finite; a program needn't handle non-finite values.
Results may differ from a plain program's by a relative error of at most 0.0007.
Values sent between devices are 32-bit elements; how exact they have to be, the bound alone decides.
A program may use at most 128 MiB of HBM per device.

v0:
```python
import jax
import jax.numpy as jnp
from jax import lax
from jax.sharding import PartitionSpec as P

K = 1024


def damped_solve(factor, columns):
    halfway = jax.scipy.linalg.solve_triangular(factor, columns, lower=True)
    return jax.scipy.linalg.solve_triangular(factor, halfway, lower=True, trans=1)


def summed_gram(sketch):
    gram = lax.dot_general(
        sketch, sketch, (((0,), (0,)), ((), ())), precision=lax.Precision.HIGHEST
    )
    summed = lax.psum(gram, ("dp", "query"))
    return summed


def on_device(hidden_acts, out_grads, loss_mask, proj_in, proj_out, queries):
    seq_count, seq_tokens, hidden_width = hidden_acts.shape
    model_width = out_grads.shape[2]
    gathered = lax.all_gather(queries, "query", axis=0, tiled=True)
    is_live = loss_mask.astype(jnp.float32)
    local_count = jnp.sum(is_live)
    act_proj = lax.dot_general(
        hidden_acts.reshape(-1, hidden_width),
        proj_in,
        (((1,), (1,)), ((), ())),
        preferred_element_type=jnp.float32,
    ).reshape(seq_count, seq_tokens, proj_in.shape[0])
    grad_proj = lax.dot_general(
        out_grads.reshape(-1, model_width),
        proj_out,
        (((1,), (1,)), ((), ())),
        preferred_element_type=jnp.float32,
    ).reshape(seq_count, seq_tokens, proj_out.shape[0])
    weighted = grad_proj * is_live[:, :, None]
    outer = jnp.einsum("stg,stx->sgx", weighted, act_proj, precision=lax.Precision.HIGHEST).reshape(
        seq_count, K
    )
    token_total = lax.psum(local_count, ("dp", "query"))
    sketch = outer / token_total
    fisher = summed_gram(sketch)
    damping = 0.1 * jnp.trace(fisher) / K
    system = fisher + damping * jnp.eye(K, dtype=jnp.float32)
    factor = jnp.linalg.cholesky(system)
    solved = damped_solve(factor, gathered.T)
    return jnp.dot(sketch, solved, precision=lax.Precision.HIGHEST)


def solution(mesh):
    return jax.shard_map(
        on_device,
        mesh=mesh,
        in_specs=(
            P(("dp", "query"), None, None),
            P(("dp", "query"), None, None),
            P(("dp", "query"), None),
            P(),
            P(),
            P("query", None),
        ),
        out_specs=P(("dp", "query"), None),
        check_vma=False,
    )
```

profile of v0, /device:TPU:0, one launch (start us, length us, event | category | flops | bytes accessed | tf_op | source)
XLA Modules:
  0.0 592.2 jit_solution(1688117754814115581)
XLA Ops:
  7.4 0.8 convert_element_type.4
  8.1 1.3 convert_reduce_fusion
  9.4 3.9 fusion.3
  13.5 10.9 %fusion = f32[64,4,32]{0,2,1:T(8,128)S(1)} fusion(bf16[64,4,14336]{2,1,0:T(4,128)(2,1)} %param.6, bf16[32,14336]{1,0:T(8,128)(2,1)S(1)} %copy-done), kind=kOutput, calls=%fused_computation.2 | convolution fusion | flops 234881024 | bytes 8290304 | tf_op jit(solution)/shard_map/dot_general | solution.py:28
  24.6 42.5 %psum.14 = f32[]{:T(128)} all-reduce(f32[]{:T(128)} %convert_reduce_fusion), channel_id=1, replica_groups=mesh['dp'=16,'query'=2] {'dp','query'}, use_global_device_ids=true, to_apply=%region_1.0 | all-reduce | flops 1 | bytes 8 | tf_op jit(solution)/shard_map/psum | solution.py:44
  67.0 2.6 convolution_divide_fusion
  70.2 5.0 fusion.103
  75.8 141.4 %all-reduce.3.cloned.1.call-done = f32[1024,1024]{0,1:T(8,128)} async-done(((f32[1024,1024]{0,1:T(8,128)}), f32[1024,1024]{0,1:T(8,128)}) %all-reduce.3.cloned.1.call-update) | async-done | bytes 4194320 | tf_op jit(solution)/shard_map/psum | solution.py:18
  217.2 2.9 select_reduce_fusion
  220.8 4.8 select_add_fusion
  225.6 5.3 copy.29
  230.9 4.5 fusion.2
  235.4 1.9 copy-done.3
  237.3 11.7 %cholesky.222 = f32[128,128]{1,0:T(8,128)S(1)} custom-call(f32[128,128]{1,0:T(8,128)S(1)} %cholesky.577), custom_call_target="Cholesky" | custom-call | tf_op jit(solution)/shard_map/jit(cholesky)/cholesky | solution.py:49
  249.1 9.8 %custom-call.66 = f32[1,128,128]{1,2,0:T(8,128)S(1)} custom-call(f32[1,128,128]{2,1,0:T(8,128)S(1)} %get-tuple-element.61), custom_call_target="InvertDiagBlocksLowerTriangular" | custom-call | tf_op jit(solution)/shard_map/jit(cholesky)/cholesky | solution.py:49
  258.9 1.5 fusion.28
  260.4 1.6 convolution_subtract_fusion
  262.3 11.7 %cholesky.243 = f32[128,128]{1,0:T(8,128)S(1)} custom-call(f32[128,128]{1,0:T(8,128)S(1)} %cholesky.581), custom_call_target="Cholesky" | custom-call | tf_op jit(solution)/shard_map/jit(cholesky)/cholesky | solution.py:49
  274.0 8.8 %copy.32 = f32[128,128]{0,1:T(8,128)S(1)} copy(f32[128,128]{1,0:T(8,128)S(1)} %cholesky.243) | data formatting | bytes 131072 | tf_op jit(solution)/shard_map/jit(cholesky)/cholesky | solution.py:49
  282.9 9.8 %custom-call.67 = f32[1,128,128]{1,2,0:T(8,128)S(1)} custom-call(f32[1,128,128]{2,1,0:T(8,128)S(1)} %get-tuple-element.59), custom_call_target="InvertDiagBlocksLowerTriangular" | custom-call | tf_op jit(solution)/shard_map/jit(cholesky)/cholesky | solution.py:49
  293.8 2.0 copy-done.1
  295.8 2.4 convolution_subtract_fusion.1
  298.2 11.7 %cholesky.466 = f32[128,128]{1,0:T(8,128)S(1)} custom-call(f32[128,128]{1,0:T(8,128)S(1)} %cholesky.586), custom_call_target="Cholesky" | custom-call | tf_op jit(solution)/shard_map/jit(cholesky)/cholesky | solution.py:49
  310.7 9.8 %custom-call.68 = f32[1,128,128]{1,2,0:T(8,128)S(1)} custom-call(f32[1,128,128]{2,1,0:T(8,128)S(1)} %get-tuple-element.57), custom_call_target="InvertDiagBlocksLowerTriangular" | custom-call | tf_op jit(solution)/shard_map/jit(cholesky)/cholesky | solution.py:49
  320.5 1.3 convolution_dynamic-update-slice_fusion.1
  321.7 3.3 convolution_subtract_fusion.2
  325.1 11.7 %cholesky.485 = f32[128,128]{1,0:T(8,128)S(1)} custom-call(f32[128,128]{1,0:T(8,128)S(1)} %cholesky.591), custom_call_target="Cholesky" | custom-call | tf_op jit(solution)/shard_map/jit(cholesky)/cholesky | solution.py:49
  337.6 9.8 %custom-call.69 = f32[1,128,128]{1,2,0:T(8,128)S(1)} custom-call(f32[1,128,128]{2,1,0:T(8,128)S(1)} %get-tuple-element.55), custom_call_target="InvertDiagBlocksLowerTriangular" | custom-call | tf_op jit(solution)/shard_map/jit(cholesky)/cholesky | solution.py:49
  347.4 1.1 convolution_dynamic-update-slice_fusion.2
  348.5 3.2 convolution_subtract_fusion.3
  351.7 12.2 %cholesky.504 = f32[128,128]{1,0:T(8,128)S(1)} custom-call(f32[128,128]{1,0:T(8,128)S(1)} %cholesky.596), custom_call_target="Cholesky" | custom-call | tf_op jit(solution)/shard_map/jit(cholesky)/cholesky | solution.py:49
  364.6 9.8 %custom-call.70 = f32[1,128,128]{1,2,0:T(8,128)S(1)} custom-call(f32[1,128,128]{2,1,0:T(8,128)S(1)} %get-tuple-element.53), custom_call_target="InvertDiagBlocksLowerTriangular" | custom-call | tf_op jit(solution)/shard_map/jit(cholesky)/cholesky | solution.py:49
  374.5 1.1 convolution_dynamic-update-slice_fusion.3
  375.6 3.1 convolution_subtract_fusion.4
  378.7 11.7 %cholesky.524 = f32[128,128]{1,0:T(8,128)S(1)} custom-call(f32[128,128]{1,0:T(8,128)S(1)} %cholesky.601), custom_call_target="Cholesky" | custom-call | tf_op jit(solution)/shard_map/jit(cholesky)/cholesky | solution.py:49
  391.1 9.8 %custom-call.71 = f32[1,128,128]{1,2,0:T(8,128)S(1)} custom-call(f32[1,128,128]{2,1,0:T(8,128)S(1)} %get-tuple-element.51), custom_call_target="InvertDiagBlocksLowerTriangular" | custom-call | tf_op jit(solution)/shard_map/jit(cholesky)/cholesky | solution.py:49
  401.0 1.0 convolution_dynamic-update-slice_fusion.5
  401.9 2.8 convolution_subtract_fusion.17
  404.8 11.7 %cholesky.544 = f32[128,128]{1,0:T(8,128)S(1)} custom-call(f32[128,128]{1,0:T(8,128)S(1)} %cholesky.606), custom_call_target="Cholesky" | custom-call | tf_op jit(solution)/shard_map/jit(cholesky)/cholesky | solution.py:49
  417.3 9.8 %custom-call.72 = f32[1,128,128]{1,2,0:T(8,128)S(1)} custom-call(f32[1,128,128]{2,1,0:T(8,128)S(1)} %get-tuple-element.49), custom_call_target="InvertDiagBlocksLowerTriangular" | custom-call | tf_op jit(solution)/shard_map/jit(cholesky)/cholesky | solution.py:49
  427.1 0.9 convolution_dynamic-update-slice_fusion.6
  428.1 2.1 convolution_subtract_fusion.20
  430.1 11.7 %cholesky.562 = f32[128,128]{1,0:T(8,128)S(1)} custom-call(f32[128,128]{1,0:T(8,128)S(1)} %convolution_subtract_fusion.20), custom_call_target="Cholesky" | custom-call | tf_op jit(solution)/shard_map/jit(cholesky)/cholesky | solution.py:49
  442.0 0.7 compare_reduce_fusion.5
  452.3 4.8 select_select_fusion
  457.2 23.7 %while.1 = (s32[]{:T(128)}, f32[1024,1024]{0,1:T(8,128)}, s32[8,2]{0,1:T(2,128)S(1)}, f32[8,128,128]{2,1,0:T(8,128)S(1)}, s32[]{:T(128)}) while((s32[]{:T(128)}, f32[1024,1024]{0,1:T(8,128)}, s32[8,2]{0,1:T(2,128)S(1)}, f32[8,128,128]{2,1,0:T(8,128)S(1)}, s32[]{:T(128)}) %tuple.50), condition=%wide.while_cond, body=%wide.while_body.sunk | while | flops 2 | bytes 393321 | solution.py:11
  457.8 2.2 dynamic-slice.7
  460.8 2.2 dynamic-slice.7
  463.7 2.2 dynamic-slice.7
  466.7 2.2 dynamic-slice.7
  469.7 2.2 dynamic-slice.7
  472.7 2.2 dynamic-slice.7
  475.7 2.2 dynamic-slice.7
  478.6 2.2 dynamic-slice.7
  480.9 78.8 %custom-call.73 = f32[8,128,128]{1,2,0:T(8,128)S(1)} custom-call(f32[8,128,128]{2,1,0:T(8,128)S(1)} %get-tuple-element.12), custom_call_target="InvertDiagBlocksLowerTriangular" | custom-call | tf_op jit(solution)/shard_map/jit(_solve_triangular)/triangular_solve | solution.py:11
  559.8 1.4 constant_dynamic-update-slice_fusion.10
  561.1 1.3 convolution_subtract_fusion.16
  562.8 1.6 convolution_subtract_fusion.12
  564.7 1.8 convolution_subtract_fusion.11
  566.9 1.9 convolution_subtract_fusion.10
  569.1 2.2 convolution_subtract_fusion.9
  571.6 2.3 convolution_subtract_fusion.15
  574.2 2.6 convolution_subtract_fusion.19
  582.7 1.7 fusion.104
  (133 shorter events, 24.9 us)
Async XLA Ops:
  7.4 6.1 %copy-start = (bf16[32,14336]{1,0:T(8,128)(2,1)S(1)}, bf16[32,14336]{1,0:T(8,128)(2,1)}, u32[]{:S(2)}) copy-start(bf16[32,14336]{1,0:T(8,128)(2,1)} %param.9) | copy-start | bytes 2752516
  7.4 209.8 %all-reduce.3.cloned.1.call-start = ((), (), s32[]{:S(2)}) async-start(), calls=%async_computation | async-start | bytes 8388608 | tf_op jit(solution)/shard_map/psum | solution.py:18
  75.2 484.5 %all-gather.2.cloned.1.call-start = ((), (), s32[]{:S(2)}) async-start(), calls=%async_computation.1 | async-start | bytes 1572864 | tf_op jit(solution)/shard_map/all_gather | solution.py:25
  235.4 1.9 copy-start.3
  293.8 2.0 copy-start.1
  559.8 7.1 %copy-start.2 = (f32[1024,1024]{0,1:T(8,128)S(1)}, f32[1024,1024]{0,1:T(8,128)}, u32[]{:S(2)}) copy-start(f32[1024,1024]{0,1:T(8,128)} %get-tuple-element.127) | copy-start | bytes 12582916
Sparse Core Ops, SparseCore 0:
  75.4 141.7 all-reduce.2
Sparse Core Ops, SparseCore 1:
  77.3 9.0 all-gather.1
where the time goes:
time: 601 us; the launch traced here: 592 us
  other arithmetic  266 us (44%)
  waiting for transfers between devices  142 us (24%)
  matrix products  72.2 us (12%)
  local copies, waits for them, and re-layouts  48 us (8%)
  blocking collectives  42.5 us (7%)
  between operations  21.6 us (4%)
    another operation x30, other arithmetic, on_device(): factor = jnp.linalg.cholesky(system)  168 us
    psum x1, waiting for transfers between devices, summed_gram(): summed = lax.psum(gram, ('dp', 'query'))  141 us
    another operation x3, other arithmetic, damped_solve(): jax.scipy.linalg.solve_triangular(factor, halfway, lower=True, trans=1)  83.6 us
    psum x1, blocking collectives, on_device(): token_total = lax.psum(local_count, ('dp', 'query'))  42.5 us
    another operation x14, matrix products, on_device(): factor = jnp.linalg.cholesky(system)  25.9 us
    another operation x40, local copies, waits for them, and re-layouts  23.5 us
    another operation x15, matrix products, damped_solve(): halfway = jax.scipy.linalg.solve_triangular(factor, columns, lower=True)  17.2 us
    another operation x25, local copies, waits for them, and re-layouts, on_device(): factor = jnp.linalg.cholesky(system)  14.1 us
  transfers between devices with their start and end apart: 2, of which 1 were waited for; matrix products, arithmetic and copies ran while one was open for 56% of the time, Pallas kernels for 0%

commit v1 on v0

v1 whole, which is shorter than its diff:
```python
import functools

import jax
import jax.numpy as jnp
from jax import lax
from jax.experimental import pallas as pl
from jax.experimental.pallas import tpu as pltpu
from jax.sharding import PartitionSpec as P

BLOCK = 128
SUB = 8
HIGHEST = lax.Precision.HIGHEST
NN = (((1,), (0,)), ((), ()))
NT = (((1,), (1,)), ((), ()))


def dot(a, b, dims=NN):
    return lax.dot_general(a, b, dims, precision=HIGHEST, preferred_element_type=jnp.float32)


def negated_inverse(block):
    size = block.shape[0]
    tiles = size // SUB
    rows = [block[SUB * t:SUB * (t + 1), :] for t in range(tiles)]
    lane = lax.broadcasted_iota(jnp.int32, (SUB, size), 1)
    sub = lax.broadcasted_iota(jnp.int32, (SUB, size), 0)

    def spread(x, at):
        return jnp.broadcast_to(x[:, at:at + 1], (SUB, size))

    for t in range(tiles):
        first = SUB * t
        inside = (lane >= first) & (lane < first + SUB)
        columns = [spread(rows[t], first + i) for i in range(SUB)]
        panel = jnp.where(inside, jnp.where(lane - first == sub, -1.0, 0.0), rows[t])
        for i in range(SUB):
            pivot = jnp.broadcast_to(columns[i][i:i + 1, :], (SUB, size))
            inverse = 1.0 / pivot
            at_pivot = sub == i

            def eliminate(x):
                scaled = jnp.broadcast_to(x[i:i + 1, :], (SUB, size)) * inverse
                return jnp.where(at_pivot, scaled, x - columns[i] * scaled)

            panel = eliminate(panel)
            for j in range(i + 1, SUB):
                columns[j] = eliminate(columns[j])
        spread_panel = [jnp.broadcast_to(panel[i:i + 1, :], (SUB, size)) for i in range(SUB)]
        updated = []
        for u in range(tiles):
            if u == t:
                updated.append(panel)
                continue
            terms = [spread(rows[u], first + i) * spread_panel[i] for i in range(SUB)]
            while len(terms) > 1:
                terms = [terms[i] + terms[i + 1] for i in range(0, len(terms), 2)]
            updated.append(jnp.where(inside, 0.0, rows[u]) - terms[0])
        rows = updated
    return jnp.concatenate(rows, axis=0)


def solve_kernel(fisher_ref, sketch_ref, queries_ref, scores_ref, work, solved):
    width = fisher_ref.shape[0]
    blocks = width // BLOCK
    work[:width, :] = fisher_ref[...]
    work[width:, :] = sketch_ref[...]
    diagonal = (lax.broadcasted_iota(jnp.int32, (BLOCK, BLOCK), 0)
                == lax.broadcasted_iota(jnp.int32, (BLOCK, BLOCK), 1))
    spans = [pl.ds(b * BLOCK, BLOCK) for b in range(blocks)]
    kept = jnp.zeros((BLOCK, BLOCK), jnp.float32)
    for span in spans:
        kept = kept + jnp.where(diagonal, work[span, span], 0.0)
    damping = 0.1 * jnp.sum(kept) / width

    @pl.loop(0, blocks)
    def _(k):
        start = pl.multiple_of(k * BLOCK, BLOCK)
        here = pl.ds(start, BLOCK)
        block = work[here, here]
        inverse = -negated_inverse(jnp.where(diagonal, block + damping, block))
        for b in range(blocks):
            @pl.when(k == b)
            def _():
                below = (b + 1) * BLOCK
                panel = work[below:, spans[b]]
                scaled = dot(panel, inverse)
                work[below:, spans[b]] = scaled
                for left in range(below, width, 2 * BLOCK):
                    right = min(left + 2 * BLOCK, width)
                    work[left:, left:right] -= dot(
                        scaled[left - below:, :], panel[left - below:right - below, :], NT)

    solved[:, spans[-1]] = work[width:, spans[-1]]
    for b in range(blocks - 2, -1, -1):
        above = (b + 1) * BLOCK
        solved[:, spans[b]] = work[width:, spans[b]] - dot(
            solved[:, above:], work[above:width, spans[b]])
    scores_ref[...] = dot(solved[...], queries_ref[...], NT)


def solve_scores(fisher, sketch, queries):
    width = fisher.shape[0]
    rows = sketch.shape[0]
    whole = pl.BlockSpec(memory_space=pltpu.VMEM)
    return pl.pallas_call(
        solve_kernel,
        out_shape=jax.ShapeDtypeStruct((rows, queries.shape[0]), jnp.float32),
        in_specs=[whole] * 3,
        out_specs=whole,
        scratch_shapes=[
            pltpu.VMEM((width + rows, width), jnp.float32),
            pltpu.VMEM((rows, width), jnp.float32),
        ],
        compiler_params=pltpu.CompilerParams(vmem_limit_bytes=48 * 2**20),
        name="solve_scores",
    )(fisher, sketch, queries)


def on_device(axes, hidden_acts, out_grads, loss_mask, proj_in, proj_out, queries):
    seq_count, seq_tokens, hidden_width = hidden_acts.shape
    model_width = out_grads.shape[2]
    gathered = lax.all_gather(queries, "query", axis=0, tiled=True)
    is_live = loss_mask.astype(jnp.float32)
    local_count = jnp.sum(is_live)
    act_proj = lax.dot_general(
        hidden_acts.reshape(-1, hidden_width),
        proj_in,
        (((1,), (1,)), ((), ())),
        preferred_element_type=jnp.float32,
    ).reshape(seq_count, seq_tokens, proj_in.shape[0])
    grad_proj = lax.dot_general(
        out_grads.reshape(-1, model_width),
        proj_out,
        (((1,), (1,)), ((), ())),
        preferred_element_type=jnp.float32,
    ).reshape(seq_count, seq_tokens, proj_out.shape[0])
    weighted = grad_proj * is_live[:, :, None]
    outer = jnp.einsum("stg,stx->sgx", weighted, act_proj, precision=HIGHEST).reshape(
        seq_count, -1
    )
    token_total = lax.psum(local_count, axes)
    sketch = outer / token_total
    gram = lax.dot_general(sketch, sketch, (((0,), (0,)), ((), ())), precision=HIGHEST)
    fisher = lax.psum(gram, axes)
    return solve_scores(fisher, sketch, gathered)


def solution(mesh):
    return jax.shard_map(
        functools.partial(on_device, ("dp", "query")),
        mesh=mesh,
        in_specs=(
            P(("dp", "query"), None, None),
            P(("dp", "query"), None, None),
            P(("dp", "query"), None),
            P(),
            P(),
            P("query", None),
        ),
        out_specs=P(("dp", "query"), None),
        check_vma=False,
    )
```

time: 601 us -> 279 us (0.46); the launches traced: 592 us -> 278 us
  other arithmetic: 266 us -> 1.97 us
  matrix products: 72.2 us -> 22.6 us
  Pallas kernels: 0 us -> 49.6 us
  local copies, waits for them, and re-layouts: 48 us -> 4.5 us
  between operations: 21.6 us -> 14.9 us
    another operation x33 -> x0, other arithmetic: 251 us -> none  [the longest x30 168 us: on_device(): factor = jnp.linalg.cholesky(system)]
    pallas_call x0 -> x1, Pallas kernels: none -> 49.6 us  [solve_scores(): pl.pallas_call(solve_kernel, out_shape=jax.ShapeDtypeStruct((rows, querie...]
    another operation x44 -> x0, matrix products: 48.2 us -> none  [the longest x14 25.9 us: on_device(): factor = jnp.linalg.cholesky(system)]
    another operation x70 -> x0, local copies, waits for them, and re-layouts: 37.6 us -> none
  transfers between devices with their start and end apart: 2 -> 2, of which waited for: 1 -> 1; matrix products, arithmetic and copies ran while one was open for 56% -> 9% of each run, Pallas kernels for 0% -> 0%
where the time goes in v1:
time: 279 us; the launch traced here: 278 us
  waiting for transfers between devices  142 us (51%)
  Pallas kernels  49.6 us (18%)
  blocking collectives  42.4 us (15%)
  matrix products  22.6 us (8%)
  between operations  14.9 us (5%)
  local copies, waits for them, and re-layouts  4.5 us (2%)
    psum x1, waiting for transfers between devices, on_device(): fisher = lax.psum(gram, axes)  141 us
    pallas_call x1, Pallas kernels, solve_scores(): pl.pallas_call(solve_kernel, out_shape=jax.ShapeDtypeStruct((rows, querie...  49.6 us
    psum x1, blocking collectives, on_device(): token_total = lax.psum(local_count, axes)  42.4 us
    dot_general x1, matrix products, on_device(): lax.dot_general(hidden_acts.reshape(-1, hidden_width), proj_in, (((1,), (...  10.9 us
  transfers between devices with their start and end apart: 2, of which 1 were waited for; matrix products, arithmetic and copies ran while one was open for 9% of the time, Pallas kernels for 0%

profile of v1, /device:TPU:0, one launch (start us, length us, event | category | flops | bytes accessed | tf_op | source)
XLA Modules:
  0.0 278.2 jit_solution(11548952572013708449)
XLA Ops:
  7.4 0.0 copy-start
  7.4 0.0 all-gather.2.cloned.1.call-start
  7.4 0.7 all-gather.2.cloned.1.call-update
  8.1 0.0 all-reduce.2.cloned.1.call-start
  8.1 0.7 convert_element_type.3
  8.8 1.3 convert_reduce_fusion
  10.1 3.9 %fusion.2 = f32[64,4,32]{0,2,1:T(8,128)S(1)} fusion(bf16[64,4,4096]{2,1,0:T(4,128)(2,1)} %param.7, bf16[32,4096]{1,0:T(8,128)(2,1)} %param.10), kind=kOutput, calls=%fused_computation.2 | convolution fusion | flops 67108864 | bytes 2392064 | tf_op jit(solution)/shard_map/dot_general | solution.py:131
  14.0 0.1 copy.12
  14.1 42.4 %psum.14 = f32[]{:T(128)} all-reduce(f32[]{:T(128)} %convert_reduce_fusion), channel_id=1, replica_groups=mesh['dp'=16,'query'=2] {'dp','query'}, use_global_device_ids=true, to_apply=%region_1.0 | all-reduce | flops 1 | bytes 8 | tf_op jit(solution)/shard_map/psum | solution.py:141
  56.6 0.0 copy-done
  56.6 10.9 %fusion = f32[64,4,32]{0,2,1:T(8,128)S(1)} fusion(bf16[64,4,14336]{2,1,0:T(4,128)(2,1)} %param.6, bf16[32,14336]{1,0:T(8,128)(2,1)S(1)} %copy-done), kind=kOutput, calls=%fused_computation | convolution fusion | flops 234881024 | bytes 8290304 | tf_op jit(solution)/shard_map/dot_general | solution.py:125
  67.5 0.1 copy.14
  67.6 0.1 copy.8
  67.7 2.6 convolution_divide_fusion
  70.3 0.6 copy.9
  70.9 5.2 %fusion.8 = f32[1024,1024]{1,0:T(8,128)} fusion(f32[64,1024]{0,1:T(8,128)S(1)} %bitcast.10), kind=kOutput, calls=%fused_computation.10 | convolution fusion | flops 805306368 | bytes 4456448 | tf_op jit(solution)/shard_map/dot_general | solution.py:143
  76.1 0.0 all-reduce.2.cloned.1.call-update
  76.1 0.2 copy.10.sketch_ref
  76.3 0.0 all-gather.2.cloned.1.call-done.queries_ref
  76.3 141.4 %all-reduce.2.cloned.1.call-done.fisher_ref = f32[1024,1024]{1,0:T(8,128)} async-done(((f32[1024,1024]{1,0:T(8,128)}), f32[1024,1024]{1,0:T(8,128)}) %all-reduce.2.cloned.1.call-update) | async-done | bytes 4194320 | tf_op jit(solution)/shard_map/psum | solution.py:144
  217.7 0.0 copy-start.1
  217.7 2.2 copy-done.1
  219.9 0.0 copy-start.2
  219.9 1.2 copy-done.2
  221.1 49.6 %solve_scores.1 = f32[64,256]{1,0:T(8,128)} custom-call(f32[1024,1024]{1,0:T(8,128)S(1)} %copy-done.1, f32[64,1024]{1,0:T(8,128)S(1)} %copy.10.sketch_ref, f32[256,1024]{1,0:T(8,128)S(1)} %copy-done.2), custom_call_target="tpu_custom_call" | custom-call | tf_op jit(solution)/shard_map/solve_scores/pallas_call | solution.py:105
Async XLA Ops:
  7.4 49.2 %copy-start = (bf16[32,14336]{1,0:T(8,128)(2,1)S(1)}, bf16[32,14336]{1,0:T(8,128)(2,1)}, u32[]{:S(2)}) copy-start(bf16[32,14336]{1,0:T(8,128)(2,1)} %param.9) | copy-start | bytes 2752516
  7.4 68.9 %all-gather.2.cloned.1.call-start = ((), (), s32[]{:S(2)}) async-start(), calls=%async_computation.1 | async-start | bytes 1572864 | tf_op jit(solution)/shard_map/all_gather | solution.py:122
  8.1 209.6 %all-reduce.2.cloned.1.call-start = ((), (), s32[]{:S(2)}) async-start(), calls=%async_computation | async-start | bytes 8388608 | tf_op jit(solution)/shard_map/psum | solution.py:144
  217.7 2.2 copy-start.1
  219.9 1.2 copy-start.2
Sparse Core Ops, SparseCore 0:
  9.7 11.7 all-gather.1
Sparse Core Ops, SparseCore 1:
  76.2 141.5 all-reduce.1

commit v2 on v1

--- a/solution.py
+++ b/solution.py
@@ -9,13 +9,28 @@
 
 BLOCK = 128
 SUB = 8
+LANES = 128
+TOKENS = 4
+MOST_GATHERED = 64
 HIGHEST = lax.Precision.HIGHEST
 NN = (((1,), (0,)), ((), ()))
 NT = (((1,), (1,)), ((), ()))
 
 
-def dot(a, b, dims=NN):
-    return lax.dot_general(a, b, dims, precision=HIGHEST, preferred_element_type=jnp.float32)
+def dot(a, b, dims=NN, precision=HIGHEST):
+    return lax.dot_general(a, b, dims, precision=precision, preferred_element_type=jnp.float32)
+
+
+def halves_of(x):
+    high = x.astype(jnp.bfloat16)
+    return high, (x - high.astype(jnp.float32)).astype(jnp.bfloat16)
+
+
+def three_products(x, y=None):
+    x_high, x_low = halves_of(x)
+    y_high, y_low = (x_high, x_low) if y is None else halves_of(y)
+    return (jnp.concatenate([x_high, x_high, x_low], axis=1),
+            jnp.concatenate([y_high, y_low, y_high], axis=1))
 
 
 def negated_inverse(block):
@@ -61,9 +76,13 @@
 
 def solve_kernel(fisher_ref, sketch_ref, queries_ref, scores_ref, work, solved):
     width = fisher_ref.shape[0]
-    blocks = width // BLOCK
     work[:width, :] = fisher_ref[...]
     work[width:, :] = sketch_ref[...]
+    eliminate(width, queries_ref, scores_ref, work, solved, 1.0)
+
+
+def eliminate(width, queries_ref, scores_ref, work, solved, factor):
+    blocks = width // BLOCK
     diagonal = (lax.broadcasted_iota(jnp.int32, (BLOCK, BLOCK), 0)
                 == lax.broadcasted_iota(jnp.int32, (BLOCK, BLOCK), 1))
     spans = [pl.ds(b * BLOCK, BLOCK) for b in range(blocks)]
@@ -85,17 +104,20 @@
                 panel = work[below:, spans[b]]
                 scaled = dot(panel, inverse)
                 work[below:, spans[b]] = scaled
+                if below == width:
+                    return
+                tall, wide = three_products(scaled, panel[:width - below, :])
                 for left in range(below, width, 2 * BLOCK):
                     right = min(left + 2 * BLOCK, width)
                     work[left:, left:right] -= dot(
-                        scaled[left - below:, :], panel[left - below:right - below, :], NT)
+                        tall[left - below:, :], wide[left - below:right - below, :], NT, None)
 
     solved[:, spans[-1]] = work[width:, spans[-1]]
     for b in range(blocks - 2, -1, -1):
         above = (b + 1) * BLOCK
         solved[:, spans[b]] = work[width:, spans[b]] - dot(
             solved[:, above:], work[above:width, spans[b]])
-    scores_ref[...] = dot(solved[...], queries_ref[...], NT)
+    scores_ref[...] = dot(solved[...], queries_ref[...], NT) * factor
 
 
 def solve_scores(fisher, sketch, queries):
@@ -116,38 +138,197 @@
     )(fisher, sketch, queries)
 
 
-def on_device(axes, hidden_acts, out_grads, loss_mask, proj_in, proj_out, queries):
+NAMES = ("dp", "query")
+
+
+def gather_kernel(dims, mine_ref, slots_ref, own_sem, send_sem, recv_sem):
+    n = len(dims)
+    dp, core = lax.axis_index("dp"), lax.axis_index("query")
+    bits = [lax.rem(lax.div(dp, d), 2) for d in dims]
+    partners = [dp + d - 2 * d * bit for d, bit in zip(dims, bits)]
+    everyone = [{"dp": p, "query": core} for p in partners] + [{"dp": dp, "query": 1 - core}]
+
+    barrier = pltpu.get_barrier_semaphore()
+    for device in everyone:
+        pl.semaphore_signal(barrier, inc=1, device_id=device, device_id_type=pl.DeviceIdType.MESH)
+    own = pltpu.make_async_copy(mine_ref, slots_ref.at[(core, *bits)], own_sem)
+    own.start()
+    own.wait()
+    pl.semaphore_wait(barrier, len(everyone))
+
+    count = [0]
+    copies = []
+
+    def send(index, device):
+        part = slots_ref.at[index]
+        at = count[0]
+        count[0] += 1
+        copy = pltpu.make_async_remote_copy(
+            src_ref=part, dst_ref=part, send_sem=send_sem.at[at], recv_sem=recv_sem.at[at],
+            device_id=device, device_id_type=pl.DeviceIdType.MESH)
+        copy.start()
+        copies.append(copy)
+        return copy
+
+    def forward(index):
+        return send(index, everyone[-1])
+
+    every = slice(None)
+    siblings = [forward((core, *bits))]
+    held = list(bits)
+    for a in range(n - 2):
+        send((core, *held), everyone[a]).wait_recv()
+        came = list(held)
+        came[a] = 1 - bits[a]
+        siblings.append(forward((core, *came)))
+        held[a] = every
+    halves = [(0, (n - 2, n - 1)), (1, (n - 1, n - 2))]
+    helds = []
+    for half, _ in halves:
+        one = list(held)
+        one[0] = half
+        helds.append(one)
+    for turn in range(2):
+        flying = [send((core, *helds[h]), everyone[order[turn]]) for h, order in halves]
+        for (h, order), copy in zip(halves, flying):
+            copy.wait_recv()
+            axis = order[turn]
+            came = list(helds[h])
+            came[axis] = 1 - bits[axis]
+            siblings.append(forward((core, *came)))
+            helds[h][axis] = every
+    for copy in siblings:
+        copy.wait_recv()
+    for copy in copies:
+        copy.wait_send()
+
+
+def gather_blocks(block, dp_size):
+    dims = []
+    d = dp_size // 2
+    while d:
+        dims.append(d)
+        d //= 2
+    n = len(dims)
+    transfers = 2 * (n - 2 + 4) + 1
+    anywhere = pl.BlockSpec(memory_space=pl.ANY)
+    return pl.pallas_call(
+        functools.partial(gather_kernel, tuple(dims)),
+        out_shape=jax.ShapeDtypeStruct((2,) + (2,) * n + block.shape, block.dtype),
+        in_specs=[anywhere],
+        out_specs=anywhere,
+        scratch_shapes=[
+            pltpu.SemaphoreType.DMA,
+            pltpu.SemaphoreType.DMA((transfers,)),
+            pltpu.SemaphoreType.DMA((transfers,)),
+        ],
+        compiler_params=pltpu.CompilerParams(collective_id=0, has_side_effects=True),
+        name="gather_tokens",
+    )(block)
+
+
+def pair_sketch(first, second, in_width, out_width):
+    lanes = 2 * LANES
+    low = lax.broadcasted_iota(jnp.int32, (in_width + out_width, LANES), 1) < LANES // 2
+    total = None
+    for start in range(0, lanes, LANES):
+        one, two = first[:, start:start + LANES], second[:, start:start + LANES]
+        for token in (jnp.where(low, one, pltpu.roll(two, LANES // 2, 1)),
+                      jnp.where(low, pltpu.roll(one, LANES // 2, 1), two)):
+            acts = token[out_width:, :]
+            term = [token[g:g + 1, :] * acts for g in range(out_width)]
+            total = term if total is None else [t + u for t, u in zip(total, term)]
+    return total
+
+
+def whole_kernel(in_width, out_width, mine_ref, slots_ref, queries_ref, scores_ref,
+                 work, solved, sketches):
+    width = in_width * out_width
+    rows = in_width + out_width
+    devices = slots_ref.shape[0]
+    per_turn = sketches.shape[1] // (LANES // 2)
+
+    def fill(first, second, column):
+        parts = pair_sketch(first, second, in_width, out_width)
+        for g, part in enumerate(parts):
+            sketches[g * in_width:(g + 1) * in_width, column:column + LANES] = part
+
+    work[:width, :] = jnp.zeros((width, width), jnp.float32)
+
+    @pl.loop(0, devices // per_turn)
+    def _(turn):
+        for p in range(0, per_turn, 2):
+            fill(slots_ref[turn * per_turn + p, :rows, :],
+                 slots_ref[turn * per_turn + p + 1, :rows, :], p // 2 * LANES)
+        tall, wide = three_products(sketches[...])
+        for left in range(0, width, 2 * BLOCK):
+            right = left + 2 * BLOCK
+            work[left:width, left:right] += dot(tall[left:, :], wide[left:right, :], NT, None)
+
+    mine = mine_ref[:rows, :]
+    fill(mine, mine, 0)
+    own = solved.shape[0]
+    work[width:, :] = sketches[:, :LANES].T[:own, :]
+    live = jnp.sum(slots_ref[:, rows:rows + 1, :])
+    eliminate(width, queries_ref, scores_ref, work, solved, live)
+
+
+def gathered_scores(block, slots, queries, in_width, out_width):
+    width = in_width * out_width
+    own = block.shape[1] // TOKENS
+    vmem = pl.BlockSpec(memory_space=pltpu.VMEM)
+    return pl.pallas_call(
+        functools.partial(whole_kernel, in_width, out_width),
+        out_shape=jax.ShapeDtypeStruct((own, queries.shape[0]), jnp.float32),
+        in_specs=[vmem] * 3,
+        out_specs=vmem,
+        scratch_shapes=[
+            pltpu.VMEM((width + own, width), jnp.float32),
+            pltpu.VMEM((own, width), jnp.float32),
+            pltpu.VMEM((width, 2 * LANES), jnp.float32),
+        ],
+        compiler_params=pltpu.CompilerParams(vmem_limit_bytes=48 * 2**20),
+        name="gathered_scores",
+    )(block, slots, queries)
+
+
+def on_device(sizes, hidden_acts, out_grads, loss_mask, proj_in, proj_out, queries):
+    dp_size, query_size = sizes
     seq_count, seq_tokens, hidden_width = hidden_acts.shape
-    model_width = out_grads.shape[2]
+    in_width, out_width = proj_in.shape[0], proj_out.shape[0]
     gathered = lax.all_gather(queries, "query", axis=0, tiled=True)
     is_live = loss_mask.astype(jnp.float32)
-    local_count = jnp.sum(is_live)
-    act_proj = lax.dot_general(
-        hidden_acts.reshape(-1, hidden_width),
-        proj_in,
-        (((1,), (1,)), ((), ())),
-        preferred_element_type=jnp.float32,
-    ).reshape(seq_count, seq_tokens, proj_in.shape[0])
-    grad_proj = lax.dot_general(
-        out_grads.reshape(-1, model_width),
-        proj_out,
-        (((1,), (1,)), ((), ())),
-        preferred_element_type=jnp.float32,
-    ).reshape(seq_count, seq_tokens, proj_out.shape[0])
-    weighted = grad_proj * is_live[:, :, None]
-    outer = jnp.einsum("stg,stx->sgx", weighted, act_proj, precision=HIGHEST).reshape(
-        seq_count, -1
-    )
-    token_total = lax.psum(local_count, axes)
-    sketch = outer / token_total
+    doubling = dp_size & (dp_size - 1) == 0 and dp_size >= 8 and query_size == 2
+    if (doubling and dp_size * query_size <= MOST_GATHERED and seq_tokens == TOKENS
+            and seq_count == LANES // 2):
+        project = functools.partial(
+            lax.dot_general, dimension_numbers=(((1,), (2,)), ((), ())),
+            preferred_element_type=jnp.float32)
+        live = is_live.T[None]
+        acts = project(proj_in, hidden_acts).transpose(0, 2, 1)
+        grads = project(proj_out, out_grads).transpose(0, 2, 1) * live
+        packed = jnp.concatenate(
+            [grads, acts, jnp.broadcast_to(live, (SUB, *live.shape[1:]))], axis=0)
+        block = packed.reshape(in_width + out_width + SUB, seq_tokens * seq_count)
+        slots = gather_blocks(block, dp_size).reshape(-1, *block.shape)
+        return gathered_scores(block, slots, gathered, in_width, out_width)
+    tokens = (seq_count * seq_tokens, -1)
+    project = functools.partial(
+        lax.dot_general, dimension_numbers=(((1,), (1,)), ((), ())),
+        preferred_element_type=jnp.float32)
+    act_proj = project(hidden_acts.reshape(tokens), proj_in)
+    grad_proj = project(out_grads.reshape(tokens), proj_out)
+    act_proj = act_proj.reshape(seq_count, seq_tokens, in_width)
+    weighted = grad_proj.reshape(seq_count, seq_tokens, out_width) * is_live[:, :, None]
+    outer = jnp.einsum("stg,stx->sgx", weighted, act_proj, precision=HIGHEST)
+    sketch = outer.reshape(seq_count, -1) / lax.psum(jnp.sum(is_live), NAMES)
     gram = lax.dot_general(sketch, sketch, (((0,), (0,)), ((), ())), precision=HIGHEST)
-    fisher = lax.psum(gram, axes)
-    return solve_scores(fisher, sketch, gathered)
+    return solve_scores(lax.psum(gram, NAMES), sketch, gathered)
 
 
 def solution(mesh):
     return jax.shard_map(
-        functools.partial(on_device, ("dp", "query")),
+        functools.partial(on_device, (mesh.shape["dp"], mesh.shape["query"])),
         mesh=mesh,
         in_specs=(
             P(("dp", "query"), None, None),

time: 279 us -> 122 us (0.44)
  waiting for transfers between devices: 142 us -> 0.73 us
  blocking collectives: 42.4 us -> 0 us
  Pallas kernels: 49.6 us -> 89 us
  matrix products: 22.6 us -> 14.1 us
    psum x1 -> x0, waiting for transfers between devices: 141 us -> none  [on_device(): fisher = lax.psum(gram, axes)]
    psum x1 -> x0, blocking collectives: 42.4 us -> none  [on_device(): token_total = lax.psum(local_count, axes)]
    pallas_call x1 -> x2, Pallas kernels: 49.6 us -> 89 us  [the longest x1 59.2 us: gathered_scores(): pl.pallas_call(functools.partial(whole_kernel, in_width, out_width), out_...]
    dot_general x4 -> x2, matrix products: 22.6 us -> 14.1 us  [the longest x1 10.9 us: on_device(): acts = project(proj_in, hidden_acts).transpose(0, 2, 1)]
  transfers between devices with their start and end apart: 2 -> 1, of which waited for: 1 -> 0; matrix products, arithmetic and copies ran while one was open for 9% -> 13% of each run, Pallas kernels for 0% -> 24%
where the time goes in v2:
time: 122 us
  Pallas kernels  89 us (73%)
  matrix products  14.1 us (12%)
  between operations  13.5 us (11%)
  local copies, waits for them, and re-layouts  3.71 us (3%)
    pallas_call x1, Pallas kernels, gathered_scores(): pl.pallas_call(functools.partial(whole_kernel, in_width, out_width), out_...  59.2 us
    pallas_call x1, Pallas kernels, gather_blocks(): pl.pallas_call(functools.partial(gather_kernel, tuple(dims)), out_shape=j...  29.8 us
    dot_general x1, matrix products, on_device(): acts = project(proj_in, hidden_acts).transpose(0, 2, 1)  10.9 us
    dot_general x1, matrix products, on_device(): grads = project(proj_out, out_grads).transpose(0, 2, 1) * live  3.27 us
    unnamed x10, local copies, waits for them, and re-layouts  2.89 us
  transfers between devices with their start and end apart: 1, of which 0 were waited for; matrix products, arithmetic and copies ran while one was open for 13% of the time, Pallas kernels for 24%

profile of v2, /device:TPU:0, one launch (start us, length us, event | category | flops | bytes accessed | tf_op | source)
XLA Modules:
  0.0 122.0 jit_solution(17265970333605649893)
XLA Ops:
  6.5 0.0 copy-start
  6.5 0.0 copy-start.4
  6.5 0.0 all-gather.2.cloned.1.call-start
  6.5 0.7 all-gather.2.cloned.1.call-update
  7.3 0.9 convert_bitcast_fusion
  8.1 0.0 copy-done
  8.1 3.3 %fusion.10 = f32[32,4,64]{2,0,1:T(8,128)S(1)} fusion(bf16[64,4,4096]{2,1,0:T(4,128)(2,1)S(1)} %copy-done, bf16[32,4096]{1,0:T(8,128)(2,1)} %param.10, f32[4,64]{1,0:T(4,128)S(1)} %convert_bitcast_fusion), kind=kOutput, calls=%fused_computation.6 | convolution fusion | flops 67117056 | bytes 2393088 | tf_op jit(solution)/shard_map/dot_general | solution.py:309
  11.4 0.0 copy-done.4
  11.4 10.9 %fusion.4 = f32[32,4,64]{2,0,1:T(8,128)S(1)} fusion(bf16[64,4,14336]{2,1,0:T(4,128)(2,1)} %param.6, bf16[32,14336]{1,0:T(8,128)(2,1)S(1)} %copy-done.4), kind=kOutput, calls=%fused_computation.4 | convolution fusion | flops 234881024 | bytes 8290304 | tf_op jit(solution)/shard_map/dot_general | solution.py:308
  22.4 0.8 reshape.7.mine_ref
  23.1 0.0 copy-start.3
  23.1 29.8 %gather_tokens.1 = f32[2,2,2,2,2,72,256]{6,5,4,3,2,1,0:T(8,128)} custom-call(f32[72,256]{1,0:T(8,128)} %reshape.7.mine_ref), custom_call_target="tpu_custom_call" | custom-call | tf_op jit(solution)/shard_map/gather_tokens/pallas_call | solution.py:215
  53.0 0.0 all-gather.2.cloned.1.call-done.queries_ref
  53.0 0.0 copy-done.3
  53.0 0.0 copy-start.1
  53.0 1.7 %copy-done.1 = f32[2,2,2,2,2,72,256]{6,5,4,3,2,1,0:T(8,128)S(1)} copy-done((f32[2,2,2,2,2,72,256]{6,5,4,3,2,1,0:T(8,128)S(1)}, f32[2,2,2,2,2,72,256]{6,5,4,3,2,1,0:T(8,128)}, u32[]{:S(2)}) %copy-start.1) | copy-done | bytes 2359320
  54.7 0.0 copy-start.2
  54.7 1.2 %copy-done.2 = f32[256,1024]{1,0:T(8,128)S(1)} copy-done((f32[256,1024]{1,0:T(8,128)S(1)}, f32[256,1024]{1,0:T(8,128)}, u32[]{:S(2)}) %copy-start.2) | copy-done | bytes 1048600
  55.9 59.2 %gathered_scores.1 = f32[64,256]{1,0:T(8,128)} custom-call(f32[72,256]{1,0:T(8,128)S(1)} %copy-done.3, f32[32,72,256]{2,1,0:T(8,128)S(1)} %bitcast.15, f32[256,1024]{1,0:T(8,128)S(1)} %copy-done.2), custom_call_target="tpu_custom_call" | custom-call | tf_op jit(solution)/shard_map/gathered_scores/pallas_call | solution.py:280
  (3 shorter events, 0.1 us)
Async XLA Ops:
  6.5 1.6 %copy-start = (bf16[64,4,4096]{2,1,0:T(4,128)(2,1)S(1)}, bf16[64,4,4096]{2,1,0:T(4,128)(2,1)}, u32[]{:S(2)}) copy-start(bf16[64,4,4096]{2,1,0:T(4,128)(2,1)} %param.7) | copy-start | bytes 6291460
  6.5 4.9 %copy-start.4 = (bf16[32,14336]{1,0:T(8,128)(2,1)S(1)}, bf16[32,14336]{1,0:T(8,128)(2,1)}, u32[]{:S(2)}) copy-start(bf16[32,14336]{1,0:T(8,128)(2,1)} %param.9) | copy-start | bytes 2752516
  6.5 46.4 %all-gather.2.cloned.1.call-start = ((), (), s32[]{:S(2)}) async-start(), calls=%async_computation | async-start | bytes 1572864 | tf_op jit(solution)/shard_map/all_gather | solution.py:299
  23.1 29.8 %copy-start.3 = (f32[72,256]{1,0:T(8,128)S(1)}, f32[72,256]{1,0:T(8,128)}, u32[]{:S(2)}) copy-start(f32[72,256]{1,0:T(8,128)} %reshape.7.mine_ref) | copy-start | bytes 221188
  53.0 1.7 %copy-start.1 = (f32[2,2,2,2,2,72,256]{6,5,4,3,2,1,0:T(8,128)S(1)}, f32[2,2,2,2,2,72,256]{6,5,4,3,2,1,0:T(8,128)}, u32[]{:S(2)}) copy-start(f32[2,2,2,2,2,72,256]{6,5,4,3,2,1,0:T(8,128)} %gather_tokens.1) | copy-start | bytes 7077892
  54.7 1.2 %copy-start.2 = (f32[256,1024]{1,0:T(8,128)S(1)}, f32[256,1024]{1,0:T(8,128)}, u32[]{:S(2)}) copy-start(f32[256,1024]{1,0:T(8,128)} %all-gather.2.cloned.1.call-done.queries_ref) | copy-start | bytes 3145732
Sparse Core Ops, SparseCore 0:
  8.9 11.7 all-gather.1

commit v3 on v2

--- a/solution.py
+++ b/solution.py
@@ -33,6 +33,13 @@
             jnp.concatenate([y_high, y_low, y_high], axis=1))
 
 
+def dot3(x, y):
+    x_high, x_low = halves_of(x)
+    y_high, y_low = halves_of(y)
+    return dot(jnp.concatenate([x_high, x_high, x_low], axis=1),
+               jnp.concatenate([y_high, y_low, y_high], axis=0), NN, None)
+
+
 def negated_inverse(block):
     size = block.shape[0]
     tiles = size // SUB
@@ -43,24 +50,31 @@
     def spread(x, at):
         return jnp.broadcast_to(x[:, at:at + 1], (SUB, size))
 
+    def across(x, at):
+        return jnp.broadcast_to(x[at:at + 1, :], (SUB, size))
+
     for t in range(tiles):
         first = SUB * t
         inside = (lane >= first) & (lane < first + SUB)
         columns = [spread(rows[t], first + i) for i in range(SUB)]
         panel = jnp.where(inside, jnp.where(lane - first == sub, -1.0, 0.0), rows[t])
-        for i in range(SUB):
-            pivot = jnp.broadcast_to(columns[i][i:i + 1, :], (SUB, size))
-            inverse = 1.0 / pivot
-            at_pivot = sub == i
-
-            def eliminate(x):
-                scaled = jnp.broadcast_to(x[i:i + 1, :], (SUB, size)) * inverse
-                return jnp.where(at_pivot, scaled, x - columns[i] * scaled)
-
-            panel = eliminate(panel)
-            for j in range(i + 1, SUB):
-                columns[j] = eliminate(columns[j])
-        spread_panel = [jnp.broadcast_to(panel[i:i + 1, :], (SUB, size)) for i in range(SUB)]
+        for i in range(0, SUB, 2):
+            p, q = columns[i], columns[i + 1]
+            a, b, c = across(p, i), across(p, i + 1), across(q, i + 1)
+            inverse = 1.0 / (a * c - b * b)
+            at_first, at_second = sub == i, sub == i + 1
+
+            def eliminate_pair(x):
+                u, v = across(x, i), across(x, i + 1)
+                first_row = (c * u - b * v) * inverse
+                second_row = (a * v - b * u) * inverse
+                rest = (x - p * first_row) - q * second_row
+                return jnp.where(at_first, first_row, jnp.where(at_second, second_row, rest))
+
+            panel = eliminate_pair(panel)
+            for j in range(i + 2, SUB):
+                columns[j] = eliminate_pair(columns[j])
+        spread_panel = [across(panel, i) for i in range(SUB)]
         updated = []
         for u in range(tiles):
             if u == t:
@@ -89,20 +103,23 @@
     kept = jnp.zeros((BLOCK, BLOCK), jnp.float32)
     for span in spans:
         kept = kept + jnp.where(diagonal, work[span, span], 0.0)
-    damping = 0.1 * jnp.sum(kept) / width
+    damping = jnp.full((BLOCK, BLOCK), 0.1 * jnp.sum(kept) / width)
+    per_damping = 1.0 / damping
 
     @pl.loop(0, blocks)
     def _(k):
         start = pl.multiple_of(k * BLOCK, BLOCK)
         here = pl.ds(start, BLOCK)
         block = work[here, here]
-        inverse = -negated_inverse(jnp.where(diagonal, block + damping, block))
+        scaled_block = block * per_damping
+        inverse = -per_damping * negated_inverse(
+            jnp.where(diagonal, scaled_block + 1.0, scaled_block))
         for b in range(blocks):
             @pl.when(k == b)
             def _():
                 below = (b + 1) * BLOCK
                 panel = work[below:, spans[b]]
-                scaled = dot(panel, inverse)
+                scaled = dot3(panel, inverse)
                 work[below:, spans[b]] = scaled
                 if below == width:
                     return
@@ -115,9 +132,10 @@
     solved[:, spans[-1]] = work[width:, spans[-1]]
     for b in range(blocks - 2, -1, -1):
         above = (b + 1) * BLOCK
-        solved[:, spans[b]] = work[width:, spans[b]] - dot(
+        solved[:, spans[b]] = work[width:, spans[b]] - dot3(
             solved[:, above:], work[above:width, spans[b]])
-    scores_ref[...] = dot(solved[...], queries_ref[...], NT) * factor
+    tall, wide = three_products(solved[...], queries_ref[...])
+    scores_ref[...] = dot(tall, wide, NT, None) * factor
 
 
 def solve_scores(fisher, sketch, queries):
@@ -241,8 +259,8 @@
     return total
 
 
-def whole_kernel(in_width, out_width, mine_ref, slots_ref, queries_ref, scores_ref,
-                 work, solved, sketches):
+def whole_kernel(in_width, out_width, mine_ref, slots_hbm, queries_hbm, scores_ref,
+                 work, solved, sketches, slots_ref, queries_ref, slot_sems, query_sem):
     width = in_width * out_width
     rows = in_width + out_width
     devices = slots_ref.shape[0]
@@ -253,10 +271,19 @@
         for g, part in enumerate(parts):
             sketches[g * in_width:(g + 1) * in_width, column:column + LANES] = part
 
+    def slot_copy(turn):
+        part = pl.ds(turn * per_turn, per_turn)
+        return pltpu.make_async_copy(slots_hbm.at[part], slots_ref.at[part], slot_sems.at[turn])
+
+    for turn in range(devices // per_turn):
+        slot_copy(turn).start()
+    query_copy = pltpu.make_async_copy(queries_hbm, queries_ref, query_sem)
+    query_copy.start()
     work[:width, :] = jnp.zeros((width, width), jnp.float32)
 
     @pl.loop(0, devices // per_turn)
     def _(turn):
+        slot_copy(turn).wait()
         for p in range(0, per_turn, 2):
             fill(slots_ref[turn * per_turn + p, :rows, :],
                  slots_ref[turn * per_turn + p + 1, :rows, :], p // 2 * LANES)
@@ -270,22 +297,28 @@
     own = solved.shape[0]
     work[width:, :] = sketches[:, :LANES].T[:own, :]
     live = jnp.sum(slots_ref[:, rows:rows + 1, :])
+    query_copy.wait()
     eliminate(width, queries_ref, scores_ref, work, solved, live)
 
 
 def gathered_scores(block, slots, queries, in_width, out_width):
     width = in_width * out_width
     own = block.shape[1] // TOKENS
+    per_turn = 4
     vmem = pl.BlockSpec(memory_space=pltpu.VMEM)
     return pl.pallas_call(
         functools.partial(whole_kernel, in_width, out_width),
         out_shape=jax.ShapeDtypeStruct((own, queries.shape[0]), jnp.float32),
-        in_specs=[vmem] * 3,
+        in_specs=[vmem, pl.BlockSpec(memory_space=pl.ANY), pl.BlockSpec(memory_space=pl.ANY)],
         out_specs=vmem,
         scratch_shapes=[
             pltpu.VMEM((width + own, width), jnp.float32),
             pltpu.VMEM((own, width), jnp.float32),
-            pltpu.VMEM((width, 2 * LANES), jnp.float32),
+            pltpu.VMEM((width, per_turn * LANES // 2), jnp.float32),
+            pltpu.VMEM(slots.shape, jnp.float32),
+            pltpu.VMEM(queries.shape, jnp.float32),
+            pltpu.SemaphoreType.DMA((slots.shape[0] // per_turn,)),
+            pltpu.SemaphoreType.DMA,
         ],
         compiler_params=pltpu.CompilerParams(vmem_limit_bytes=48 * 2**20),
         name="gathered_scores",

time: 122 us -> 119 us (0.975)
  Pallas kernels: 89 us -> 86 us
    pallas_call x1, Pallas kernels: 59.2 us -> 56.2 us  [gathered_scores(): pl.pallas_call(functools.partial(whole_kernel, in_width, out_width), out_...]
  transfers between devices with their start and end apart: 1 -> 1, of which waited for: 0 -> 0; matrix products, arithmetic and copies ran while one was open for 13% -> 13% of each run, Pallas kernels for 24% -> 25%
where the time goes in v3:
time: 119 us
  Pallas kernels  86 us (72%)
  matrix products  14.1 us (12%)
  between operations  13.5 us (11%)
  local copies, waits for them, and re-layouts  3.71 us (3%)
    pallas_call x1, Pallas kernels, gathered_scores(): pl.pallas_call(functools.partial(whole_kernel, in_width, out_width), out_...  56.2 us
    pallas_call x1, Pallas kernels, gather_blocks(): pl.pallas_call(functools.partial(gather_kernel, tuple(dims)), out_shape=j...  29.8 us
    dot_general x1, matrix products, on_device(): acts = project(proj_in, hidden_acts).transpose(0, 2, 1)  10.9 us
    dot_general x1, matrix products, on_device(): grads = project(proj_out, out_grads).transpose(0, 2, 1) * live  3.27 us
    unnamed x10, local copies, waits for them, and re-layouts  2.89 us
  transfers between devices with their start and end apart: 1, of which 0 were waited for; matrix products, arithmetic and copies ran while one was open for 13% of the time, Pallas kernels for 25%

profile of v3, /device:TPU:0, one launch (start us, length us, event | category | flops | bytes accessed | tf_op | source)
XLA Modules:
  0.0 118.9 jit_solution(13144576162466274503)
XLA Ops:
  6.5 0.0 copy-start
  6.5 0.0 copy-start.4
  6.5 0.0 all-gather.2.cloned.1.call-start
  6.5 0.7 all-gather.2.cloned.1.call-update
  7.3 0.9 convert_bitcast_fusion
  8.1 0.0 copy-done
  8.1 3.3 %fusion.10 = f32[32,4,64]{2,0,1:T(8,128)S(1)} fusion(bf16[64,4,4096]{2,1,0:T(4,128)(2,1)S(1)} %copy-done, bf16[32,4096]{1,0:T(8,128)(2,1)} %param.10, f32[4,64]{1,0:T(4,128)S(1)} %convert_bitcast_fusion), kind=kOutput, calls=%fused_computation.6 | convolution fusion | flops 67117056 | bytes 2393088 | tf_op jit(solution)/shard_map/dot_general | solution.py:342
  11.4 0.0 copy-done.4
  11.4 10.9 %fusion.4 = f32[32,4,64]{2,0,1:T(8,128)S(1)} fusion(bf16[64,4,14336]{2,1,0:T(4,128)(2,1)} %param.6, bf16[32,14336]{1,0:T(8,128)(2,1)S(1)} %copy-done.4), kind=kOutput, calls=%fused_computation.4 | convolution fusion | flops 234881024 | bytes 8290304 | tf_op jit(solution)/shard_map/dot_general | solution.py:341
  22.4 0.8 reshape.7.mine_ref
  23.1 0.0 copy-start.3
  23.1 29.8 %gather_tokens.1 = f32[2,2,2,2,2,72,256]{6,5,4,3,2,1,0:T(8,128)} custom-call(f32[72,256]{1,0:T(8,128)} %reshape.7.mine_ref), custom_call_target="tpu_custom_call" | custom-call | tf_op jit(solution)/shard_map/gather_tokens/pallas_call | solution.py:233
  53.0 0.0 all-gather.2.cloned.1.call-done.queries_hbm
  53.0 0.0 copy-done.3
  53.0 0.0 copy-start.1
  53.0 1.7 %copy-done.1 = f32[2,2,2,2,2,72,256]{6,5,4,3,2,1,0:T(8,128)S(1)} copy-done((f32[2,2,2,2,2,72,256]{6,5,4,3,2,1,0:T(8,128)S(1)}, f32[2,2,2,2,2,72,256]{6,5,4,3,2,1,0:T(8,128)}, u32[]{:S(2)}) %copy-start.1) | copy-done | bytes 2359320
  54.7 0.0 copy-start.2
  54.7 1.2 %copy-done.2 = f32[256,1024]{1,0:T(8,128)S(1)} copy-done((f32[256,1024]{1,0:T(8,128)S(1)}, f32[256,1024]{1,0:T(8,128)}, u32[]{:S(2)}) %copy-start.2) | copy-done | bytes 1048600
  55.9 56.2 %gathered_scores.1 = f32[64,256]{1,0:T(8,128)} custom-call(f32[72,256]{1,0:T(8,128)S(1)} %copy-done.3, f32[32,72,256]{2,1,0:T(8,128)S(1)} %bitcast.15, f32[256,1024]{1,0:T(8,128)S(1)} %copy-done.2), custom_call_target="tpu_custom_call" | custom-call | tf_op jit(solution)/shard_map/gathered_scores/pallas_call | solution.py:309
  (3 shorter events, 0.1 us)
Async XLA Ops:
  6.5 1.6 %copy-start = (bf16[64,4,4096]{2,1,0:T(4,128)(2,1)S(1)}, bf16[64,4,4096]{2,1,0:T(4,128)(2,1)}, u32[]{:S(2)}) copy-start(bf16[64,4,4096]{2,1,0:T(4,128)(2,1)} %param.7) | copy-start | bytes 6291460
  6.5 4.9 %copy-start.4 = (bf16[32,14336]{1,0:T(8,128)(2,1)S(1)}, bf16[32,14336]{1,0:T(8,128)(2,1)}, u32[]{:S(2)}) copy-start(bf16[32,14336]{1,0:T(8,128)(2,1)} %param.9) | copy-start | bytes 2752516
  6.5 46.4 %all-gather.2.cloned.1.call-start = ((), (), s32[]{:S(2)}) async-start(), calls=%async_computation | async-start | bytes 1572864 | tf_op jit(solution)/shard_map/all_gather | solution.py:332
  23.1 29.8 %copy-start.3 = (f32[72,256]{1,0:T(8,128)S(1)}, f32[72,256]{1,0:T(8,128)}, u32[]{:S(2)}) copy-start(f32[72,256]{1,0:T(8,128)} %reshape.7.mine_ref) | copy-start | bytes 221188
  53.0 1.7 %copy-start.1 = (f32[2,2,2,2,2,72,256]{6,5,4,3,2,1,0:T(8,128)S(1)}, f32[2,2,2,2,2,72,256]{6,5,4,3,2,1,0:T(8,128)}, u32[]{:S(2)}) copy-start(f32[2,2,2,2,2,72,256]{6,5,4,3,2,1,0:T(8,128)} %gather_tokens.1) | copy-start | bytes 7077892
  54.7 1.2 %copy-start.2 = (f32[256,1024]{1,0:T(8,128)S(1)}, f32[256,1024]{1,0:T(8,128)}, u32[]{:S(2)}) copy-start(f32[256,1024]{1,0:T(8,128)} %all-gather.2.cloned.1.call-done.queries_hbm) | copy-start | bytes 3145732
Sparse Core Ops, SparseCore 0:
  8.9 11.7 all-gather.1
